TPU v7x, 32 devices: a whole 2x2x4 slice. The times are simulated.
32 devices in a mesh: row: 4 (over z), col: 8 (over y, x, core).
Axes of the slice: x: 2, y: 2, z: 4, core: 2. Of those that a mesh axis runs over, the one named last changes fastest.
Arguments:
- blocks: bfloat16 [64, 8, 128, 128], P(('row', 'col')), may hold values from -1.5 to 1.5
- colidx: int32 [64, 8], P(('row', 'col')), may hold values from 0 to 63, as said below
- counts: int32 [4, 8], P('row', 'col'), may hold values from 1 to 66, as said below
- out_list: int32 [4, 8, 66], P('row', 'col'), may hold values from 0 to 65, as said below
Outputs:
- packed: bfloat16 [2112, 128, 128], P(('row', 'col'))
- offsets: int32 [4, 8], P('row', 'col')
Inputs may be any that keep to these rules, and one draw needn't show every extreme that they name: `colidx`: block row i names 8 distinct block columns (i + e) mod 64 with -8 <= e <= 8; among them are i, (i - 8) mod 64 and (i + 8) mod 64. `counts`: some device keeps all 66 blocks and some device keeps one. `out_list`: each device's list is an ordering of 0 to 65; only its first counts entries are used.
All inputs are finite; a program needn't handle non-finite values.
Results may differ from a plain program's by a relative error of at most 0.001.
Values may be sent and summed in bfloat16 or wider, within the bound.
A program may use at most 64 MiB of HBM per device.

v0:
```python
import jax
import jax.numpy as jnp
from jax import lax
from jax.sharding import PartitionSpec as P

H = 8


def shifted(x, axis, by):
    length = lax.axis_size(axis)
    return lax.ppermute(x, axis, [(i, (i + by) % length) for i in range(length)])


def carried_in(part, axis, combine, identity):
    place = lax.axis_index(axis)
    gathered = lax.all_gather(part, axis)
    state = jnp.zeros_like(part) + jnp.asarray(identity, part.dtype)

    def one(hop, state):
        return combine(state, lax.dynamic_index_in_dim(gathered, hop, 0, False))

    return lax.fori_loop(0, place, one, state)


def add_ints(earlier, later):
    return earlier + later


def shards(blocks, colidx, counts, out_list):
    rows_here = blocks.shape[0]
    slot_count = blocks.shape[1]
    block_size = blocks.shape[2]
    devices_all = lax.axis_size("row") * lax.axis_size("col")
    block_total = rows_here * devices_all
    device = lax.axis_index("row") * lax.axis_size("col") + lax.axis_index("col")
    first_row = device * rows_here
    side_count = (H + rows_here - 1) // rows_here
    below_pieces = []
    above_pieces = []
    lower_blocks, lower_cols = (blocks, colidx)
    upper_blocks, upper_cols = (blocks, colidx)
    for distance in range(side_count):
        lower_blocks, lower_cols = shifted((lower_blocks, lower_cols), ("row", "col"), 1)
        upper_blocks, upper_cols = shifted((upper_blocks, upper_cols), ("row", "col"), -1)
        below_pieces.append((lower_blocks, lower_cols))
        above_pieces.append((upper_blocks, upper_cols))
    ordered = list(reversed(below_pieces)) + [(blocks, colidx)] + above_pieces
    near_blocks = jnp.concatenate([piece[0] for piece in ordered], axis=0)
    near_cols = jnp.concatenate([piece[1] for piece in ordered], axis=0)
    band_size = 4 * H + 1
    row_ids = first_row + jnp.arange(rows_here, dtype=jnp.int32)
    row_range = jnp.arange(rows_here, dtype=jnp.int32)[:, None]
    local_place = (colidx - first_row + side_count * rows_here) % block_total

    def accumulate(slot_index, running):
        a_blocks = lax.dynamic_index_in_dim(blocks, slot_index, 1, keepdims=False)
        wanted = lax.dynamic_index_in_dim(local_place, slot_index, 1, keepdims=False)
        b_blocks = jnp.take(near_blocks, wanted, axis=0)
        b_cols = jnp.take(near_cols, wanted, axis=0)
        products = jnp.einsum(
            "iab,iubc->iuac", a_blocks, b_blocks, preferred_element_type=jnp.float32
        )
        places = (b_cols - row_ids[:, None] + 2 * H) % block_total
        return running.at[row_range, places].add(products)

    zero_tile = jnp.zeros((rows_here, band_size, block_size, block_size), jnp.float32)
    grid_tile = lax.fori_loop(0, slot_count, accumulate, zero_tile)
    tile_count = rows_here * band_size
    flattened = grid_tile.reshape(tile_count, block_size, block_size)
    picked = jnp.take(flattened, out_list[0, 0], axis=0)
    in_list = jnp.arange(tile_count, dtype=jnp.int32) < counts[0, 0]
    packed = jnp.where(in_list[:, None, None], picked, jnp.zeros_like(picked)).astype(jnp.bfloat16)
    zero_count = jnp.zeros((1, 1), jnp.int32)
    within = carried_in(counts, "col", add_ints, zero_count)
    row_sum = lax.psum(counts, "col")
    rows_before = carried_in(row_sum, "row", add_ints, zero_count)
    offsets = (rows_before + within).astype(jnp.int32)
    return (packed, offsets)


def solution(mesh):
    in_specs = (
        P(("row", "col"), None, None, None),
        P(("row", "col"), None),
        P("row", "col"),
        P("row", "col", None),
    )
    out_specs = (P(("row", "col"), None, None), P("row", "col"))
    return jax.shard_map(shards, mesh=mesh, in_specs=in_specs, out_specs=out_specs, check_vma=False)
```

profile of v0, /device:TPU:0, one launch (start us, length us, event | category | flops | bytes accessed | tf_op | source)
XLA Modules:
  0.0 183.6 jit_solution(10515040716581930730)
XLA Ops:
  1.1 6.0 %collective-permute-start.12 = (bf16[2,8,128,128]{3,2,1,0:T(8,128)(2,1)}, bf16[2,8,128,128]{3,2,1,0:T(8,128)(2,1)S(1)}, u32[]{:S(2)}, u32[]{:S(2)}) collective-permute-start(bf16[2,8,128,128]{3,2,1,0:T(8,128)(2,1)} %param.10), channel_id=1, source_target_pairs={{0,31},{1,0},{2,1},{3,2},{4,3},{5,4},{6,5},{7,6},{8,7},{9,8},{10,9... | collective-permute-start | bytes 1572872 | tf_op jit(solution)/shard_map/ppermute | solution.py:11
  7.1 7.1 %collective-permute-done.8 = bf16[2,8,128,128]{3,2,1,0:T(8,128)(2,1)S(1)} collective-permute-done((bf16[2,8,128,128]{3,2,1,0:T(8,128)(2,1)}, bf16[2,8,128,128]{3,2,1,0:T(8,128)(2,1)S(1)}, u32[]{:S(2)}, u32[]{:S(2)}) %collective-permute-start.8) | collective-permute-done | bytes 524320 | tf_op jit(solution)/shard_map/ppermute | solution.py:11
  14.3 1.5 collective-permute-start.9
  15.8 3.8 %collective-permute-start.13 = (bf16[2,8,128,128]{3,2,1,0:T(8,128)(2,1)S(1)}, bf16[2,8,128,128]{3,2,1,0:T(8,128)(2,1)S(1)}, u32[]{:S(2)}, u32[]{:S(2)}) collective-permute-start(bf16[2,8,128,128]{3,2,1,0:T(8,128)(2,1)S(1)} %collective-permute-done.12), channel_id=1, source_target_pairs={{0,31},{1,0},{2,1},{3,2},{4,3},{5,4},{6,5},{7,6},{8,7},{9,8},{10,9... | collective-permute-start | bytes 1572872 | tf_op jit(solution)/shard_map/ppermute | solution.py:11
  19.7 6.9 %collective-permute-done.9 = bf16[2,8,128,128]{3,2,1,0:T(8,128)(2,1)S(1)} collective-permute-done((bf16[2,8,128,128]{3,2,1,0:T(8,128)(2,1)S(1)}, bf16[2,8,128,128]{3,2,1,0:T(8,128)(2,1)S(1)}, u32[]{:S(2)}, u32[]{:S(2)}) %collective-permute-start.9) | collective-permute-done | bytes 524320 | tf_op jit(solution)/shard_map/ppermute | solution.py:11
  26.6 3.3 %collective-permute-start.10 = (bf16[2,8,128,128]{3,2,1,0:T(8,128)(2,1)S(1)}, bf16[2,8,128,128]{3,2,1,0:T(8,128)(2,1)S(1)}, u32[]{:S(2)}, u32[]{:S(2)}) collective-permute-start(bf16[2,8,128,128]{3,2,1,0:T(8,128)(2,1)S(1)} %collective-permute-done.9), channel_id=1, source_target_pairs={{0,1},{1,2},{2,3},{3,4},{4,5},{5,6},{6,7},{7,8},{8,9},{9,10},{10,1... | collective-permute-start | bytes 1572872 | tf_op jit(solution)/shard_map/ppermute | solution.py:11
  30.6 2.5 %collective-permute-start = (s32[2,8]{0,1:T(8,128)S(1)}, s32[2,8]{0,1:T(8,128)S(1)}, u32[]{:S(2)}, u32[]{:S(2)}) collective-permute-start(s32[2,8]{0,1:T(8,128)S(1)} %copy.20), channel_id=1, source_target_pairs={{0,1},{1,2},{2,3},{3,4},{4,5},{5,6},{6,7},{7,8},{8,9},{9,10},{10,1... | collective-permute-start | bytes 200 | tf_op jit(solution)/shard_map/ppermute | solution.py:11
  33.7 1.2 dynamic-slice.1
  35.7 7.3 %all-reduce.2 = (s32[1,1,1]{2,1,0:T(1,128)}, s32[8]{0:T(128)S(1)}) all-reduce(s32[1,1,1]{2,1,0:T(1,128)} %bitcast.7, s32[8]{0:T(128)S(1)} %bitcast_dynamic-update-slice_fusion), channel_id=1, replica_groups=mesh['row'=4,'col'=8] {'col'}, use_global_device_ids=true, to_apply=%region_3.4 | all-reduce | flops 9 | bytes 72 | tf_op jit(solution)/shard_map/psum | solution.py:75
  43.0 1.2 dynamic-slice
  44.3 1.3 bitcast_dynamic-update-slice_fusion.1
  45.6 3.5 %collective-permute-start.4 = (s32[2,8]{0,1:T(8,128)S(1)}, s32[2,8]{0,1:T(8,128)S(1)}, u32[]{:S(2)}, u32[]{:S(2)}) collective-permute-start(s32[2,8]{0,1:T(8,128)S(1)} %copy.20), channel_id=1, source_target_pairs={{0,31},{1,0},{2,1},{3,2},{4,3},{5,4},{6,5},{7,6},{8,7},{9,8},{10,9... | collective-permute-start | bytes 200 | tf_op jit(solution)/shard_map/ppermute | solution.py:11
  49.0 5.6 %all-reduce = s32[4]{0:T(128)S(1)} all-reduce(s32[4]{0:T(128)S(1)} %bitcast_dynamic-update-slice_fusion.1), channel_id=1, replica_groups=mesh['row'=4,'col'=8] {'row'}, use_global_device_ids=true, to_apply=%add | all-reduce | flops 4 | bytes 32
  55.3 13.6 %collective-permute-start.14 = (bf16[2,8,128,128]{3,2,1,0:T(8,128)(2,1)S(1)}, bf16[2,8,128,128]{3,2,1,0:T(8,128)(2,1)}, u32[]{:S(2)}, u32[]{:S(2)}) collective-permute-start(bf16[2,8,128,128]{3,2,1,0:T(8,128)(2,1)S(1)} %collective-permute-done.13), channel_id=1, source_target_pairs={{0,31},{1,0},{2,1},{3,2},{4,3},{5,4},{6,5},{7,6},{8,7},{9,8},{10,9... | collective-permute-start | bytes 1572872 | tf_op jit(solution)/shard_map/ppermute | solution.py:11
  69.6 5.4 %collective-permute-start.5 = (s32[2,8]{0,1:T(8,128)S(1)}, s32[2,8]{0,1:T(8,128)S(1)}, u32[]{:S(2)}, u32[]{:S(2)}) collective-permute-start(s32[2,8]{0,1:T(8,128)S(1)} %collective-permute-done.4), channel_id=1, source_target_pairs={{0,31},{1,0},{2,1},{3,2},{4,3},{5,4},{6,5},{7,6},{8,7},{9,8},{10,9... | collective-permute-start | bytes 200 | tf_op jit(solution)/shard_map/ppermute | solution.py:11
  75.0 6.2 %collective-permute-done.1 = s32[2,8]{0,1:T(8,128)S(1)} collective-permute-done((s32[2,8]{0,1:T(8,128)S(1)}, s32[2,8]{0,1:T(8,128)S(1)}, u32[]{:S(2)}, u32[]{:S(2)}) %collective-permute-start.1) | collective-permute-done | bytes 96 | tf_op jit(solution)/shard_map/ppermute | solution.py:11
  81.2 5.3 %collective-permute-start.6 = (s32[2,8]{0,1:T(8,128)S(1)}, s32[2,8]{0,1:T(8,128)S(1)}, u32[]{:S(2)}, u32[]{:S(2)}) collective-permute-start(s32[2,8]{0,1:T(8,128)S(1)} %collective-permute-done.5), channel_id=1, source_target_pairs={{0,31},{1,0},{2,1},{3,2},{4,3},{5,4},{6,5},{7,6},{8,7},{9,8},{10,9... | collective-permute-start | bytes 200 | tf_op jit(solution)/shard_map/ppermute | solution.py:11
  86.6 1.4 collective-permute-done.2
  88.0 5.3 %collective-permute-start.7 = (s32[2,8]{0,1:T(8,128)S(1)}, s32[2,8]{0,1:T(8,128)S(1)}, u32[]{:S(2)}, u32[]{:S(2)}) collective-permute-start(s32[2,8]{0,1:T(8,128)S(1)} %collective-permute-done.6), channel_id=1, source_target_pairs={{0,31},{1,0},{2,1},{3,2},{4,3},{5,4},{6,5},{7,6},{8,7},{9,8},{10,9... | collective-permute-start | bytes 200 | tf_op jit(solution)/shard_map/ppermute | solution.py:11
  93.3 1.3 collective-permute-done.3
  94.8 5.3 %collective-permute-start.15 = (bf16[2,8,128,128]{3,2,1,0:T(8,128)(2,1)}, bf16[2,8,128,128]{3,2,1,0:T(8,128)(2,1)S(1)}, u32[]{:S(2)}, u32[]{:S(2)}) collective-permute-start(bf16[2,8,128,128]{3,2,1,0:T(8,128)(2,1)} %collective-permute-done.14), channel_id=1, source_target_pairs={{0,31},{1,0},{2,1},{3,2},{4,3},{5,4},{6,5},{7,6},{8,7},{9,8},{10,9... | collective-permute-start | bytes 1572872 | tf_op jit(solution)/shard_map/ppermute | solution.py:11
  100.1 1.9 %constant_dynamic-update-slice_fusion.8 = bf16[18,8,128,128]{3,2,1,0:T(8,128)(2,1)} fusion(bf16[2,8,128,128]{3,2,1,0:T(8,128)(2,1)} %collective-permute-done.11), kind=kLoop, calls=%fused_computation.43 | loop fusion | bytes 1048576
  102.0 0.8 constant_dynamic-update-slice_fusion.7
  102.8 0.9 constant_dynamic-update-slice_fusion.6
  105.4 0.8 constant_dynamic-update-slice_fusion.3
  106.2 0.8 constant_dynamic-update-slice_fusion.2
  107.1 1.9 %constant_dynamic-update-slice_fusion.1 = bf16[18,8,128,128]{3,2,1,0:T(8,128)(2,1)} fusion(bf16[18,8,128,128]{3,2,1,0:T(8,128)(2,1)} %constant_dynamic-update-slice_fusion.2, bf16[2,8,128,128]{3,2,1,0:T(8,128)(2,1)} %collective-permute-done.14), kind=kLoop, calls=%fused_computation.36 | loop fusion | bytes 1048576
  108.9 0.8 constant_dynamic-update-slice_fusion
  109.8 2.6 %broadcast_in_dim.86 = f32[2,33,128,128]{3,2,1,0:T(8,128)} broadcast(f32[]{:T(128)} %constant.202.clone.1), dimensions={} | broadcast | bytes 4325380 | tf_op jit(solution)/shard_map/broadcast_in_dim | solution.py:66
  112.4 64.7 %while.38 = (s32[]{:T(128)}, f32[2,33,128,128]{3,2,1,0:T(8,128)}, s32[2,8]{0,1:T(8,128)S(1)}, s32[18,8]{1,0:T(8,128)S(1)}, bf16[18,8,128,128]{3,2,1,0:T(8,128)(2...) while((s32[]{:T(128)}, f32[2,33,128,128]{3,2,1,0:T(8,128)}, ...), condition=%wide.region_2.3_spmd.clone, body=%wide.region_0.2_spmd.clone.sunk | while | flops 67634568 | bytes 7935153 | solution.py:67
  113.1 3.0 %gather_fusion.1 = bf16[2,8,128,128]{3,2,1,0:T(8,128)(2,1)S(1)} fusion(bf16[18,8,128,128]{3,2,1,0:T(8,128)(2,1)} %get-tuple-element.472, s32[1024]{0:T(1024)S(1)} %pad_clamp_fusion.3), kind=kCustom, calls=%fused_computation.1.clone.clone.1 | custom fusion | bytes 1048584 | tf_op jit(solution)/shard_map/while/body/eval_jaxpr/jit(_take)/gather | solution.py:58
  116.9 3.5 %scatter_fusion = f32[2,33,128,128]{3,2,1,0:T(8,128)} fusion(f32[2,33,128,128]{3,2,1,0:T(8,128)} %get-tuple-element.461, s32[16]{0:T(128)S(1)} %reshape.250, f32[16,128,128]{2,1,0:T(8,128)S(1)} %copy.34), kind=kCustom, calls=%fused_computation.3.clone.clone.1 | custom fusion | flops 262144 | bytes 3145856 | tf_op jit(solution)/shard_map/while/body/eval_jaxpr/scatter-add | solution.py:64
  121.2 3.0 %gather_fusion.1 = bf16[2,8,128,128]{3,2,1,0:T(8,128)(2,1)S(1)} fusion(bf16[18,8,128,128]{3,2,1,0:T(8,128)(2,1)} %get-tuple-element.472, s32[1024]{0:T(1024)S(1)} %pad_clamp_fusion.3), kind=kCustom, calls=%fused_computation.1.clone.clone.1 | custom fusion | bytes 1048584 | tf_op jit(solution)/shard_map/while/body/eval_jaxpr/jit(_take)/gather | solution.py:58
  125.0 3.5 %scatter_fusion = f32[2,33,128,128]{3,2,1,0:T(8,128)} fusion(f32[2,33,128,128]{3,2,1,0:T(8,128)} %get-tuple-element.461, s32[16]{0:T(128)S(1)} %reshape.250, f32[16,128,128]{2,1,0:T(8,128)S(1)} %copy.34), kind=kCustom, calls=%fused_computation.3.clone.clone.1 | custom fusion | flops 262144 | bytes 3145856 | tf_op jit(solution)/shard_map/while/body/eval_jaxpr/scatter-add | solution.py:64
  129.3 3.0 %gather_fusion.1 = bf16[2,8,128,128]{3,2,1,0:T(8,128)(2,1)S(1)} fusion(bf16[18,8,128,128]{3,2,1,0:T(8,128)(2,1)} %get-tuple-element.472, s32[1024]{0:T(1024)S(1)} %pad_clamp_fusion.3), kind=kCustom, calls=%fused_computation.1.clone.clone.1 | custom fusion | bytes 1048584 | tf_op jit(solution)/shard_map/while/body/eval_jaxpr/jit(_take)/gather | solution.py:58
  133.1 3.5 %scatter_fusion = f32[2,33,128,128]{3,2,1,0:T(8,128)} fusion(f32[2,33,128,128]{3,2,1,0:T(8,128)} %get-tuple-element.461, s32[16]{0:T(128)S(1)} %reshape.250, f32[16,128,128]{2,1,0:T(8,128)S(1)} %copy.34), kind=kCustom, calls=%fused_computation.3.clone.clone.1 | custom fusion | flops 262144 | bytes 3145856 | tf_op jit(solution)/shard_map/while/body/eval_jaxpr/scatter-add | solution.py:64
  137.4 3.0 %gather_fusion.1 = bf16[2,8,128,128]{3,2,1,0:T(8,128)(2,1)S(1)} fusion(bf16[18,8,128,128]{3,2,1,0:T(8,128)(2,1)} %get-tuple-element.472, s32[1024]{0:T(1024)S(1)} %pad_clamp_fusion.3), kind=kCustom, calls=%fused_computation.1.clone.clone.1 | custom fusion | bytes 1048584 | tf_op jit(solution)/shard_map/while/body/eval_jaxpr/jit(_take)/gather | solution.py:58
  141.1 3.5 %scatter_fusion = f32[2,33,128,128]{3,2,1,0:T(8,128)} fusion(f32[2,33,128,128]{3,2,1,0:T(8,128)} %get-tuple-element.461, s32[16]{0:T(128)S(1)} %reshape.250, f32[16,128,128]{2,1,0:T(8,128)S(1)} %copy.34), kind=kCustom, calls=%fused_computation.3.clone.clone.1 | custom fusion | flops 262144 | bytes 3145856 | tf_op jit(solution)/shard_map/while/body/eval_jaxpr/scatter-add | solution.py:64
  145.5 3.0 %gather_fusion.1 = bf16[2,8,128,128]{3,2,1,0:T(8,128)(2,1)S(1)} fusion(bf16[18,8,128,128]{3,2,1,0:T(8,128)(2,1)} %get-tuple-element.472, s32[1024]{0:T(1024)S(1)} %pad_clamp_fusion.3), kind=kCustom, calls=%fused_computation.1.clone.clone.1 | custom fusion | bytes 1048584 | tf_op jit(solution)/shard_map/while/body/eval_jaxpr/jit(_take)/gather | solution.py:58
  149.2 3.6 %scatter_fusion = f32[2,33,128,128]{3,2,1,0:T(8,128)} fusion(f32[2,33,128,128]{3,2,1,0:T(8,128)} %get-tuple-element.461, s32[16]{0:T(128)S(1)} %reshape.250, f32[16,128,128]{2,1,0:T(8,128)S(1)} %copy.34), kind=kCustom, calls=%fused_computation.3.clone.clone.1 | custom fusion | flops 262144 | bytes 3145856 | tf_op jit(solution)/shard_map/while/body/eval_jaxpr/scatter-add | solution.py:64
  153.6 3.0 %gather_fusion.1 = bf16[2,8,128,128]{3,2,1,0:T(8,128)(2,1)S(1)} fusion(bf16[18,8,128,128]{3,2,1,0:T(8,128)(2,1)} %get-tuple-element.472, s32[1024]{0:T(1024)S(1)} %pad_clamp_fusion.3), kind=kCustom, calls=%fused_computation.1.clone.clone.1 | custom fusion | bytes 1048584 | tf_op jit(solution)/shard_map/while/body/eval_jaxpr/jit(_take)/gather | solution.py:58
  157.4 3.5 %scatter_fusion = f32[2,33,128,128]{3,2,1,0:T(8,128)} fusion(f32[2,33,128,128]{3,2,1,0:T(8,128)} %get-tuple-element.461, s32[16]{0:T(128)S(1)} %reshape.250, f32[16,128,128]{2,1,0:T(8,128)S(1)} %copy.34), kind=kCustom, calls=%fused_computation.3.clone.clone.1 | custom fusion | flops 262144 | bytes 3145856 | tf_op jit(solution)/shard_map/while/body/eval_jaxpr/scatter-add | solution.py:64
  161.7 3.0 %gather_fusion.1 = bf16[2,8,128,128]{3,2,1,0:T(8,128)(2,1)S(1)} fusion(bf16[18,8,128,128]{3,2,1,0:T(8,128)(2,1)} %get-tuple-element.472, s32[1024]{0:T(1024)S(1)} %pad_clamp_fusion.3), kind=kCustom, calls=%fused_computation.1.clone.clone.1 | custom fusion | bytes 1048584 | tf_op jit(solution)/shard_map/while/body/eval_jaxpr/jit(_take)/gather | solution.py:58
  165.4 3.6 %scatter_fusion = f32[2,33,128,128]{3,2,1,0:T(8,128)} fusion(f32[2,33,128,128]{3,2,1,0:T(8,128)} %get-tuple-element.461, s32[16]{0:T(128)S(1)} %reshape.250, f32[16,128,128]{2,1,0:T(8,128)S(1)} %copy.34), kind=kCustom, calls=%fused_computation.3.clone.clone.1 | custom fusion | flops 262144 | bytes 3145856 | tf_op jit(solution)/shard_map/while/body/eval_jaxpr/scatter-add | solution.py:64
  169.8 3.0 %gather_fusion.1 = bf16[2,8,128,128]{3,2,1,0:T(8,128)(2,1)S(1)} fusion(bf16[18,8,128,128]{3,2,1,0:T(8,128)(2,1)} %get-tuple-element.472, s32[1024]{0:T(1024)S(1)} %pad_clamp_fusion.3), kind=kCustom, calls=%fused_computation.1.clone.clone.1 | custom fusion | bytes 1048584 | tf_op jit(solution)/shard_map/while/body/eval_jaxpr/jit(_take)/gather | solution.py:58
  173.5 3.5 %scatter_fusion = f32[2,33,128,128]{3,2,1,0:T(8,128)} fusion(f32[2,33,128,128]{3,2,1,0:T(8,128)} %get-tuple-element.461, s32[16]{0:T(128)S(1)} %reshape.250, f32[16,128,128]{2,1,0:T(8,128)S(1)} %copy.34), kind=kCustom, calls=%fused_computation.3.clone.clone.1 | custom fusion | flops 262144 | bytes 3145856 | tf_op jit(solution)/shard_map/while/body/eval_jaxpr/scatter-add | solution.py:64
  177.1 3.4 %gather_fusion.2 = bf16[66,128,128]{2,1,0:T(8,128)(2,1)S(1)} fusion(f32[66,128,128]{2,1,0:T(8,128)} %bitcast.63, s32[1024]{0:T(1024)S(1)} %pad_clamp_fusion.1), kind=kCustom, calls=%fused_computation.2 | custom fusion | bytes 4325640 | tf_op jit(solution)/shard_map/jit(_take)/gather | solution.py:70
  180.4 2.0 %select_convert_fusion = bf16[66,128,128]{2,1,0:T(8,128)(2,1)} fusion(bf16[66,128,128]{2,1,0:T(8,128)(2,1)S(1)} %gather_fusion.2, pred[66]{0:T(512)(128)(4,1)S(1)} %compare_and_fusion, pred[66]{0:T(512)(128)(4,1)S(1)} %iota_compare_fusion.1), kind=kLoop, calls=%fused_computation.34 | loop fusion | flops 2162688 | bytes 4325508 | tf_op jit(solution)/shard_map/convert_element_type | solution.py:72
  (105 shorter events, 17.4 us)
Async XLA Ops:
  0.6 103.9 %copy-start = (bf16[2,8,128,128]{3,2,1,0:T(8,128)(2,1)S(1)}, bf16[2,8,128,128]{3,2,1,0:T(8,128)(2,1)}, u32[]{:S(2)}) copy-start(bf16[2,8,128,128]{3,2,1,0:T(8,128)(2,1)} %param.10) | copy-start | bytes 1572868
  0.6 13.6 %collective-permute-start.8 = (bf16[2,8,128,128]{3,2,1,0:T(8,128)(2,1)}, bf16[2,8,128,128]{3,2,1,0:T(8,128)(2,1)S(1)}, u32[]{:S(2)}, u32[]{:S(2)}) collective-permute-start(bf16[2,8,128,128]{3,2,1,0:T(8,128)(2,1)} %param.10), channel_id=1, source_target_pairs={{0,1},{1,2},{2,3},{3,4},{4,5},{5,6},{6,7},{7,8},{8,9},{9,10},{10,1... | collective-permute-start | bytes 1572872 | tf_op jit(solution)/shard_map/ppermute | solution.py:11
  1.1 14.7 %collective-permute-start.12 = (bf16[2,8,128,128]{3,2,1,0:T(8,128)(2,1)}, bf16[2,8,128,128]{3,2,1,0:T(8,128)(2,1)S(1)}, u32[]{:S(2)}, u32[]{:S(2)}) collective-permute-start(bf16[2,8,128,128]{3,2,1,0:T(8,128)(2,1)} %param.10), channel_id=1, source_target_pairs={{0,31},{1,0},{2,1},{3,2},{4,3},{5,4},{6,5},{7,6},{8,7},{9,8},{10,9... | collective-permute-start | bytes 1572872 | tf_op jit(solution)/shard_map/ppermute | solution.py:11
  14.3 12.3 %collective-permute-start.9 = (bf16[2,8,128,128]{3,2,1,0:T(8,128)(2,1)S(1)}, bf16[2,8,128,128]{3,2,1,0:T(8,128)(2,1)S(1)}, u32[]{:S(2)}, u32[]{:S(2)}) collective-permute-start(bf16[2,8,128,128]{3,2,1,0:T(8,128)(2,1)S(1)} %collective-permute-done.8), channel_id=1, source_target_pairs={{0,1},{1,2},{2,3},{3,4},{4,5},{5,6},{6,7},{7,8},{8,9},{9,10},{10,1... | collective-permute-start | bytes 1572872 | tf_op jit(solution)/shard_map/ppermute | solution.py:11
  15.8 39.5 %collective-permute-start.13 = (bf16[2,8,128,128]{3,2,1,0:T(8,128)(2,1)S(1)}, bf16[2,8,128,128]{3,2,1,0:T(8,128)(2,1)S(1)}, u32[]{:S(2)}, u32[]{:S(2)}) collective-permute-start(bf16[2,8,128,128]{3,2,1,0:T(8,128)(2,1)S(1)} %collective-permute-done.12), channel_id=1, source_target_pairs={{0,31},{1,0},{2,1},{3,2},{4,3},{5,4},{6,5},{7,6},{8,7},{9,8},{10,9... | collective-permute-start | bytes 1572872 | tf_op jit(solution)/shard_map/ppermute | solution.py:11
  26.6 42.3 %collective-permute-start.10 = (bf16[2,8,128,128]{3,2,1,0:T(8,128)(2,1)S(1)}, bf16[2,8,128,128]{3,2,1,0:T(8,128)(2,1)S(1)}, u32[]{:S(2)}, u32[]{:S(2)}) collective-permute-start(bf16[2,8,128,128]{3,2,1,0:T(8,128)(2,1)S(1)} %collective-permute-done.9), channel_id=1, source_target_pairs={{0,1},{1,2},{2,3},{3,4},{4,5},{5,6},{6,7},{7,8},{8,9},{9,10},{10,1... | collective-permute-start | bytes 1572872 | tf_op jit(solution)/shard_map/ppermute | solution.py:11
  30.6 39.0 %collective-permute-start = (s32[2,8]{0,1:T(8,128)S(1)}, s32[2,8]{0,1:T(8,128)S(1)}, u32[]{:S(2)}, u32[]{:S(2)}) collective-permute-start(s32[2,8]{0,1:T(8,128)S(1)} %copy.20), channel_id=1, source_target_pairs={{0,1},{1,2},{2,3},{3,4},{4,5},{5,6},{6,7},{7,8},{8,9},{9,10},{10,1... | collective-permute-start | bytes 200 | tf_op jit(solution)/shard_map/ppermute | solution.py:11
  45.6 24.1 %collective-permute-start.4 = (s32[2,8]{0,1:T(8,128)S(1)}, s32[2,8]{0,1:T(8,128)S(1)}, u32[]{:S(2)}, u32[]{:S(2)}) collective-permute-start(s32[2,8]{0,1:T(8,128)S(1)} %copy.20), channel_id=1, source_target_pairs={{0,31},{1,0},{2,1},{3,2},{4,3},{5,4},{6,5},{7,6},{8,7},{9,8},{10,9... | collective-permute-start | bytes 200 | tf_op jit(solution)/shard_map/ppermute | solution.py:11
  55.3 39.5 %collective-permute-start.14 = (bf16[2,8,128,128]{3,2,1,0:T(8,128)(2,1)S(1)}, bf16[2,8,128,128]{3,2,1,0:T(8,128)(2,1)}, u32[]{:S(2)}, u32[]{:S(2)}) collective-permute-start(bf16[2,8,128,128]{3,2,1,0:T(8,128)(2,1)S(1)} %collective-permute-done.13), channel_id=1, source_target_pairs={{0,31},{1,0},{2,1},{3,2},{4,3},{5,4},{6,5},{7,6},{8,7},{9,8},{10,9... | collective-permute-start | bytes 1572872 | tf_op jit(solution)/shard_map/ppermute | solution.py:11
  68.9 31.2 %collective-permute-start.11 = (bf16[2,8,128,128]{3,2,1,0:T(8,128)(2,1)S(1)}, bf16[2,8,128,128]{3,2,1,0:T(8,128)(2,1)}, u32[]{:S(2)}, u32[]{:S(2)}) collective-permute-start(bf16[2,8,128,128]{3,2,1,0:T(8,128)(2,1)S(1)} %collective-permute-done.10), channel_id=1, source_target_pairs={{0,1},{1,2},{2,3},{3,4},{4,5},{5,6},{6,7},{7,8},{8,9},{9,10},{10,1... | collective-permute-start | bytes 1572872 | tf_op jit(solution)/shard_map/ppermute | solution.py:11
  69.6 11.7 %collective-permute-start.1 = (s32[2,8]{0,1:T(8,128)S(1)}, s32[2,8]{0,1:T(8,128)S(1)}, u32[]{:S(2)}, u32[]{:S(2)}) collective-permute-start(s32[2,8]{0,1:T(8,128)S(1)} %collective-permute-done), channel_id=1, source_target_pairs={{0,1},{1,2},{2,3},{3,4},{4,5},{5,6},{6,7},{7,8},{8,9},{9,10},{10,1... | collective-permute-start | bytes 200 | tf_op jit(solution)/shard_map/ppermute | solution.py:11
  69.6 11.6 %collective-permute-start.5 = (s32[2,8]{0,1:T(8,128)S(1)}, s32[2,8]{0,1:T(8,128)S(1)}, u32[]{:S(2)}, u32[]{:S(2)}) collective-permute-start(s32[2,8]{0,1:T(8,128)S(1)} %collective-permute-done.4), channel_id=1, source_target_pairs={{0,31},{1,0},{2,1},{3,2},{4,3},{5,4},{6,5},{7,6},{8,7},{9,8},{10,9... | collective-permute-start | bytes 200 | tf_op jit(solution)/shard_map/ppermute | solution.py:11
  81.2 6.7 %collective-permute-start.2 = (s32[2,8]{0,1:T(8,128)S(1)}, s32[2,8]{0,1:T(8,128)S(1)}, u32[]{:S(2)}, u32[]{:S(2)}) collective-permute-start(s32[2,8]{0,1:T(8,128)S(1)} %collective-permute-done.1), channel_id=1, source_target_pairs={{0,1},{1,2},{2,3},{3,4},{4,5},{5,6},{6,7},{7,8},{8,9},{9,10},{10,1... | collective-permute-start | bytes 200 | tf_op jit(solution)/shard_map/ppermute | solution.py:11
  81.2 6.7 %collective-permute-start.6 = (s32[2,8]{0,1:T(8,128)S(1)}, s32[2,8]{0,1:T(8,128)S(1)}, u32[]{:S(2)}, u32[]{:S(2)}) collective-permute-start(s32[2,8]{0,1:T(8,128)S(1)} %collective-permute-done.5), channel_id=1, source_target_pairs={{0,31},{1,0},{2,1},{3,2},{4,3},{5,4},{6,5},{7,6},{8,7},{9,8},{10,9... | collective-permute-start | bytes 200 | tf_op jit(solution)/shard_map/ppermute | solution.py:11
  88.0 6.6 %collective-permute-start.3 = (s32[2,8]{0,1:T(8,128)S(1)}, s32[2,8]{0,1:T(8,128)S(1)}, u32[]{:S(2)}, u32[]{:S(2)}) collective-permute-start(s32[2,8]{0,1:T(8,128)S(1)} %collective-permute-done.2), channel_id=1, source_target_pairs={{0,1},{1,2},{2,3},{3,4},{4,5},{5,6},{6,7},{7,8},{8,9},{9,10},{10,1... | collective-permute-start | bytes 200 | tf_op jit(solution)/shard_map/ppermute | solution.py:11
  88.0 6.7 %collective-permute-start.7 = (s32[2,8]{0,1:T(8,128)S(1)}, s32[2,8]{0,1:T(8,128)S(1)}, u32[]{:S(2)}, u32[]{:S(2)}) collective-permute-start(s32[2,8]{0,1:T(8,128)S(1)} %collective-permute-done.6), channel_id=1, source_target_pairs={{0,31},{1,0},{2,1},{3,2},{4,3},{5,4},{6,5},{7,6},{8,7},{9,8},{10,9... | collective-permute-start | bytes 200 | tf_op jit(solution)/shard_map/ppermute | solution.py:11
  94.8 14.1 %collective-permute-start.15 = (bf16[2,8,128,128]{3,2,1,0:T(8,128)(2,1)}, bf16[2,8,128,128]{3,2,1,0:T(8,128)(2,1)S(1)}, u32[]{:S(2)}, u32[]{:S(2)}) collective-permute-start(bf16[2,8,128,128]{3,2,1,0:T(8,128)(2,1)} %collective-permute-done.14), channel_id=1, source_target_pairs={{0,31},{1,0},{2,1},{3,2},{4,3},{5,4},{6,5},{7,6},{8,7},{9,8},{10,9... | collective-permute-start | bytes 1572872 | tf_op jit(solution)/shard_map/ppermute | solution.py:11
where the time goes:
time: 185 us; the launch traced here: 184 us
  starting transfers between devices  56.1 us (30%)
  local copies, waits for them, and re-layouts  52.6 us (28%)
  other arithmetic  32.6 us (18%)
  waiting for transfers between devices  23 us (12%)
  blocking collectives  12.9 us (7%)
  matrix products  3.4 us (2%)
  between operations  2.5 us (1%)
    ppermute x16, starting transfers between devices, shifted(): lax.ppermute(x, axis, [(i, (i + by) % length) for i in range(length)])  56.1 us
    scatter-add x8, other arithmetic, accumulate(): return running.at[row_range, places].add(products)  28.3 us
    gather x8, local copies, waits for them, and re-layouts, accumulate(): b_blocks = jnp.take(near_blocks, wanted, axis=0)  23.9 us
    ppermute x16, waiting for transfers between devices, shifted(): lax.ppermute(x, axis, [(i, (i + by) % length) for i in range(length)])  23 us
    unnamed x18, local copies, waits for them, and re-layouts  14.1 us
    psum x1, blocking collectives, shards(): row_sum = lax.psum(counts, 'col')  7.35 us
    unnamed x1, blocking collectives  5.59 us
    gather x8, local copies, waits for them, and re-layouts, accumulate(): b_cols = jnp.take(near_cols, wanted, axis=0)  4.47 us
  transfers between devices with their start and end apart: 16, of which 5 were waited for; matrix products, arithmetic and copies ran while one was open for 8% of the time, Pallas kernels for 0%

commit v1 on v0

v1 whole, which is shorter than its diff:
```python
import functools

import jax
import jax.numpy as jnp
from jax import lax
from jax.experimental import pallas as pl
from jax.experimental.pallas import tpu as pltpu
from jax.sharding import PartitionSpec as P

H = 8
CHUNKS = 4
SIDE = 4


def exchange_kernel(rows_total, cols_total, own_ref, near_ref, send_sem, recv_sem, own_sem):
    count = rows_total * cols_total
    me = lax.axis_index("row") * cols_total + lax.axis_index("col")
    core = me % 2
    pair = me // 2
    p = pair % 4
    low = p < 2
    sign = jnp.where(low, 1, -1)
    type_a = jnp.logical_or(p == 0, p == 3)
    x_step = jnp.where(p % 2 == 0, 1, -1)
    y_step = 2 * sign

    def place(device):
        return (device // cols_total, device % cols_total)

    partner = me + 1 - 2 * core
    x_dev = me + 2 * x_step
    y_dev = me + 2 * y_step
    z_to = (me + 8 * sign + count) % count
    z_from = (me - 8 * sign + count) % count

    barrier = pltpu.get_barrier_semaphore()
    for device in (partner, x_dev, y_dev, z_to, z_from):
        pl.semaphore_signal(barrier, inc=1, device_id=place(device), device_id_type=pl.DeviceIdType.MESH)
    pl.semaphore_wait(barrier, 5)

    per = near_ref.shape[1] // CHUNKS

    def part(ref, slot, c):
        return ref.at[slot, pl.ds(c * per, per)]

    def copy(source, c, lane, device, slot):
        return pltpu.make_async_remote_copy(
            src_ref=source,
            dst_ref=part(near_ref, slot, c),
            send_sem=send_sem.at[lane, c],
            recv_sem=recv_sem.at[slot, c],
            device_id=place(device),
            device_id_type=pl.DeviceIdType.MESH,
        )

    def wait_in(slot, c):
        copy(part(near_ref, slot, c), c, 0, partner, slot).wait_recv()

    def forward(slot, c, lane, device, to_slot):
        copy(part(near_ref, slot, c), c, lane, device, to_slot).start()

    own_copy = pltpu.make_async_copy(own_ref.at[0], near_ref.at[SIDE], own_sem)
    own_copy.start()

    y_slot = SIDE + 4 * sign
    z_slot = SIDE - 4 * sign
    x_slot = SIDE + 2 * x_step
    x2_slot = SIDE - 2 * x_step
    to_partner = 2 * core - 1
    for c in range(CHUNKS):
        source = part(own_ref, 0, c)
        copy(source, c, 0, y_dev, SIDE - 4 * sign).start()
        copy(source, c, 1, x_dev, SIDE - 2 * x_step).start()
    for c in range(CHUNKS):
        copy(part(own_ref, 0, c), c, 2, partner, SIDE + to_partner).start()

    y_goes = (core == 0) == low

    def y_arrived(c):
        wait_in(y_slot, c)
        forward(y_slot, c, 3, z_to, SIDE - 4 * sign)

        @pl.when(type_a)
        def _():
            forward(y_slot, c, 4, x_dev, y_slot - 2 * x_step)

        @pl.when(y_goes)
        def _():
            forward(y_slot, c, 6, partner, y_slot + to_partner)

    def x_arrived(c):
        wait_in(x_slot, c)
        forward(x_slot, c, 5, partner, x_slot + to_partner)

    def z_arrived(c):
        wait_in(z_slot, c)

        @pl.when(jnp.logical_not(type_a))
        def _():
            forward(z_slot, c, 4, x_dev, z_slot - 2 * x_step)

        @pl.when(jnp.logical_not(y_goes))
        def _():
            forward(z_slot, c, 6, partner, z_slot + to_partner)

    def x2_arrived(c):
        wait_in(x2_slot, c)
        forward(x2_slot, c, 7, partner, x2_slot + to_partner)

    for c in range(CHUNKS):
        y_arrived(c)
        x_arrived(c)
        if c > 0:
            z_arrived(c - 1)
    z_arrived(CHUNKS - 1)
    for c in range(CHUNKS):
        x2_arrived(c)
    for c in range(CHUNKS):
        for odd in (SIDE - 3, SIDE - 1, SIDE + 1, SIDE + 3):
            wait_in(odd, c)
    own_copy.wait()
    for c in range(CHUNKS):
        for lane in range(8):
            copy(part(own_ref, 0, c), c, lane, partner, SIDE).wait_send()


def exchange(blocks, mesh_shape):
    rows_here, slots, size, _ = blocks.shape
    own = blocks.reshape(1, rows_here * slots, size, size)
    near = pl.pallas_call(
        functools.partial(exchange_kernel, *mesh_shape),
        out_shape=jax.ShapeDtypeStruct((2 * SIDE + 1,) + own.shape[1:], own.dtype),
        in_specs=[pl.BlockSpec(memory_space=pl.ANY)],
        out_specs=pl.BlockSpec(memory_space=pl.ANY),
        scratch_shapes=[
            pltpu.SemaphoreType.DMA((8, CHUNKS)),
            pltpu.SemaphoreType.DMA((2 * SIDE + 1, CHUNKS)),
            pltpu.SemaphoreType.DMA,
        ],
        compiler_params=pltpu.CompilerParams(collective_id=0, has_side_effects=True),
    )(own)
    return near


def product_kernel(count, rows_here, slots, me_ref, table_ref, list_ref, near_ref, packed_ref, offset_ref, acc_ref):
    me = me_ref[0]
    width = rows_here * slots + 1
    total = count * rows_here
    band = 4 * H + 1
    first = me * rows_here
    tiles = rows_here * band

    offset_ref[0, 0] = lax.fori_loop(0, me, lambda i, s: s + table_ref[i * width + width - 1], jnp.int32(0))

    def clear(q, carry):
        acc_ref[q] = jnp.zeros(acc_ref.shape[1:], acc_ref.dtype)
        return carry

    lax.fori_loop(0, tiles, clear, 0, unroll=2)

    def wrapped(value):
        return lax.rem(value + total, total)

    def one(step, carry):
        a = step // slots
        col = table_ref[me * width + step]
        place = wrapped(col - first + SIDE * rows_here) * slots
        left = near_ref[SIDE * rows_here * slots + step]
        base = (col // rows_here) * width + (col % rows_here) * slots
        for u in range(slots):
            f = wrapped(table_ref[base + u] - (first + a) + 2 * H)
            q = a * band + f
            acc_ref[q] += jnp.dot(left, near_ref[place + u], preferred_element_type=jnp.float32)
        return carry

    lax.fori_loop(0, rows_here * slots, one, 0)

    kept = table_ref[me * width + width - 1]

    def pack(i, carry):
        q = list_ref[i]
        value = acc_ref[q].astype(packed_ref.dtype)
        packed_ref[i] = jnp.where(i < kept, value, jnp.zeros_like(value))
        return carry

    lax.fori_loop(0, tiles, pack, 0, unroll=2)


def shards(mesh_shape, blocks, colidx, counts, out_list):
    rows_here, slots, size, _ = blocks.shape
    count = mesh_shape[0] * mesh_shape[1]
    tiles = out_list.shape[-1]
    me = (lax.axis_index("row") * mesh_shape[1] + lax.axis_index("col")).astype(jnp.int32)
    meta = jnp.concatenate([colidx.reshape(-1), counts.reshape(-1)])
    table = lax.all_gather(meta, ("row", "col"), tiled=True)
    near = exchange(blocks, mesh_shape)
    near = near.reshape(-1, size, size)
    smem = pl.BlockSpec(memory_space=pltpu.SMEM)
    vmem = pl.BlockSpec(memory_space=pltpu.VMEM)
    packed, offsets = pl.pallas_call(
        functools.partial(product_kernel, count, rows_here, slots),
        out_shape=(
            jax.ShapeDtypeStruct((tiles, size, size), jnp.bfloat16),
            jax.ShapeDtypeStruct((1, 1), jnp.int32),
        ),
        in_specs=[smem, smem, smem, vmem],
        out_specs=(vmem, smem),
        scratch_shapes=[pltpu.VMEM((tiles, size, size), jnp.float32)],
        compiler_params=pltpu.CompilerParams(vmem_limit_bytes=40 * 1024 * 1024),
    )(me.reshape(1), table, out_list.reshape(-1), near)
    return packed, offsets


def solution(mesh):
    mesh_shape = (mesh.shape["row"], mesh.shape["col"])
    in_specs = (
        P(("row", "col"), None, None, None),
        P(("row", "col"), None),
        P("row", "col"),
        P("row", "col", None),
    )
    out_specs = (P(("row", "col"), None, None), P("row", "col"))
    return jax.shard_map(
        functools.partial(shards, mesh_shape), mesh=mesh, in_specs=in_specs, out_specs=out_specs, check_vma=False
    )
```

time: 185 us -> 81.9 us (0.44)
  starting transfers between devices: 56.1 us -> 0 us
  local copies, waits for them, and re-layouts: 52.6 us -> 3.1 us
  Pallas kernels: 0 us -> 35 us
  other arithmetic: 32.6 us -> 0.16 us
  blocking collectives: 12.9 us -> 42 us
  waiting for transfers between devices: 23 us -> 0 us
  matrix products: 3.4 us -> 0 us
    ppermute x16 -> x0, starting transfers between devices: 56.1 us -> none  [shifted(): lax.ppermute(x, axis, [(i, (i + by) % length) for i in range(length)])]
    unnamed x1, blocking collectives: 5.59 us -> 42 us
    pallas_call x0 -> x2, Pallas kernels: none -> 35 us  [the longest x1 28.4 us: exchange(): pl.pallas_call(functools.partial(exchange_kernel, *mesh_shape), out_shape...]
    gather x17 -> x0, local copies, waits for them, and re-layouts: 31.7 us -> none  [the longest x8 23.9 us: accumulate(): b_blocks = jnp.take(near_blocks, wanted, axis=0)]
    scatter-add x8 -> x0, other arithmetic: 28.3 us -> none  [accumulate(): return running.at[row_range, places].add(products)]
    ppermute x16 -> x0, waiting for transfers between devices: 23 us -> none  [shifted(): lax.ppermute(x, axis, [(i, (i + by) % length) for i in range(length)])]
    unnamed x18 -> x5, local copies, waits for them, and re-layouts: 14.1 us -> 2.34 us
    psum x1 -> x0, blocking collectives: 7.35 us -> none  [shards(): row_sum = lax.psum(counts, 'col')]
  transfers between devices with their start and end apart: 16 -> 0, of which waited for: 5 -> 0; matrix products, arithmetic and copies ran while one was open for 8% -> 0% of each run, Pallas kernels for 0% -> 0%
where the time goes in v1:
time: 81.9 us; the launch traced here: 81.6 us
  blocking collectives  42 us (51%)
  Pallas kernels  35 us (43%)
  local copies, waits for them, and re-layouts  3.1 us (4%)
  between operations  1.32 us (2%)
    unnamed x1, blocking collectives  42 us
    pallas_call x1, Pallas kernels, exchange(): pl.pallas_call(functools.partial(exchange_kernel, *mesh_shape), out_shape...  28.4 us
    pallas_call x1, Pallas kernels, shards(): pl.pallas_call(functools.partial(product_kernel, count, rows_here, slots)...  6.63 us
    unnamed x5, local copies, waits for them, and re-layouts  2.34 us

profile of v1, /device:TPU:0, one launch (start us, length us, event | category | flops | bytes accessed | tf_op | source)
XLA Modules:
  0.0 81.6 jit_solution(7882481901193225058)
XLA Ops:
  0.6 0.0 copy-start.1
  1.3 0.8 reshape.23
  2.1 0.2 add_dynamic-update-slice_fusion
  2.2 42.0 %all-reduce.table_ref = s32[544]{0:T(1024)S(1)} all-reduce(s32[544]{0:T(1024)S(1)} %add_dynamic-update-slice_fusion), channel_id=1, replica_groups=mesh['row'=4,'col'=8] {'row','col'}, use_global_device_ids=true, to_apply=%add | all-reduce | flops 544 | bytes 4352
  44.2 28.4 %shard_map.59 = bf16[9,16,128,128]{3,2,1,0:T(8,128)(2,1)} custom-call(bf16[1,16,128,128]{3,2,1,0:T(8,128)(2,1)} %bitcast.8), custom_call_target="tpu_custom_call" | custom-call | tf_op jit(solution)/shard_map/pallas_call | solution.py:130
  72.6 0.0 copy-done.1
  72.6 0.0 copy-start
  72.6 2.3 %copy-done = bf16[9,16,128,128]{3,2,1,0:T(8,128)(2,1)S(1)} copy-done((bf16[9,16,128,128]{3,2,1,0:T(8,128)(2,1)S(1)}, bf16[9,16,128,128]{3,2,1,0:T(8,128)(2,1)}, u32[]{:S(2)}) %copy-start) | copy-done | bytes 4718616
  75.0 6.6 %shard_map.60 = (bf16[66,128,128]{2,1,0:T(8,128)(2,1)}, s32[1,1]{1,0:T(1,128)}) custom-call(s32[1]{0:T(128)} %bitcast.me_ref, s32[544]{0:T(1024)S(1)} %all-reduce.table_ref, s32[66]{0:T(128)S(1)} %bitcast.7, bf16[144,128,128]{2,1,0:T(8,128)(2,1)S(1)} %bitcast.6), custom_call_target="tpu_custom_call" | custom-call | tf_op jit(solution)/shard_map/pallas_call | solution.py:200
  (1 shorter events, 0.0 us)
Async XLA Ops:
  0.6 72.0 %copy-start.1 = (s32[1,1,66]{2,1,0:T(1,128)S(1)}, s32[1,1,66]{2,1,0:T(1,128)}, u32[]{:S(2)}) copy-start(s32[1,1,66]{2,1,0:T(1,128)} %param.7) | copy-start | bytes 796
  72.6 2.3 %copy-start = (bf16[9,16,128,128]{3,2,1,0:T(8,128)(2,1)S(1)}, bf16[9,16,128,128]{3,2,1,0:T(8,128)(2,1)}, u32[]{:S(2)}) copy-start(bf16[9,16,128,128]{3,2,1,0:T(8,128)(2,1)} %shard_map.59) | copy-start | bytes 14155780

commit v2 on v1

--- a/solution.py
+++ b/solution.py
@@ -12,7 +12,10 @@
 SIDE = 4
 
 
-def exchange_kernel(rows_total, cols_total, own_ref, near_ref, send_sem, recv_sem, own_sem):
+def exchange_kernel(
+    rows_total, cols_total, col_ref, count_ref, own_ref, near_ref, meta_ref,
+    table_ref, send_sem, recv_sem, own_sem, row_send, row_recv, grid_send, grid_recv,
+):
     count = rows_total * cols_total
     me = lax.axis_index("row") * cols_total + lax.axis_index("col")
     core = me % 2
@@ -34,9 +37,32 @@
     z_from = (me - 8 * sign + count) % count
 
     barrier = pltpu.get_barrier_semaphore()
-    for device in (partner, x_dev, y_dev, z_to, z_from):
-        pl.semaphore_signal(barrier, inc=1, device_id=place(device), device_id_type=pl.DeviceIdType.MESH)
-    pl.semaphore_wait(barrier, 5)
+    r, cc = me // cols_total, me % cols_total
+    row_peers = [(r, (cc + j) % cols_total) for j in range(1, cols_total)]
+    grid_peers = [((r + j) % rows_total, cc) for j in range(1, rows_total)]
+    others = [] if cols_total == 8 else [place(z_to), place(z_from)]
+    greeted = row_peers + grid_peers + others
+    for device in greeted:
+        pl.semaphore_signal(barrier, inc=1, device_id=device, device_id_type=pl.DeviceIdType.MESH)
+
+    entries = col_ref.shape[0] * col_ref.shape[1]
+    lane = lax.broadcasted_iota(jnp.int32, (1, 128), 1)
+    row = jnp.where(lane == entries, count_ref[0, 0], 0)
+    for i in range(entries):
+        row = jnp.where(lane == i, col_ref[i // col_ref.shape[1], i % col_ref.shape[1]], row)
+    table_ref[me] = row
+    pl.semaphore_wait(barrier, len(greeted))
+
+    def row_copy(j):
+        return pltpu.make_async_remote_copy(
+            src_ref=table_ref.at[me], dst_ref=table_ref.at[me], send_sem=row_send.at[j], recv_sem=row_recv.at[j],
+            device_id=row_peers[j], device_id_type=pl.DeviceIdType.MESH)
+
+    def grid_copy(j):
+        rows = table_ref.at[pl.ds(r * cols_total, cols_total)]
+        return pltpu.make_async_remote_copy(
+            src_ref=rows, dst_ref=rows, send_sem=grid_send.at[j], recv_sem=grid_recv.at[j],
+            device_id=grid_peers[j], device_id_type=pl.DeviceIdType.MESH)
 
     per = near_ref.shape[1] // CHUNKS
 
@@ -74,6 +100,13 @@
     for c in range(CHUNKS):
         copy(part(own_ref, 0, c), c, 2, partner, SIDE + to_partner).start()
 
+    for j in range(cols_total - 1):
+        row_copy(j).start()
+    for j in range(cols_total - 1):
+        row_copy(j).wait()
+    for j in range(rows_total - 1):
+        grid_copy(j).start()
+
     y_goes = (core == 0) == low
 
     def y_arrived(c):
@@ -119,71 +152,91 @@
         for odd in (SIDE - 3, SIDE - 1, SIDE + 1, SIDE + 3):
             wait_in(odd, c)
     own_copy.wait()
+    for j in range(rows_total - 1):
+        grid_copy(j).wait()
+    for k in range(2 * SIDE + 1):
+        meta_ref[k] = table_ref[(me + k - SIDE + count) % count]
+    index = lax.broadcasted_iota(jnp.int32, (count, 1, 128), 0)
+    meta_ref[2 * SIDE + 1] = jnp.sum(jnp.where(index < me, table_ref[...], 0), axis=0)
     for c in range(CHUNKS):
         for lane in range(8):
             copy(part(own_ref, 0, c), c, lane, partner, SIDE).wait_send()
 
 
-def exchange(blocks, mesh_shape):
+def exchange(blocks, colidx, counts, mesh_shape):
     rows_here, slots, size, _ = blocks.shape
     own = blocks.reshape(1, rows_here * slots, size, size)
-    near = pl.pallas_call(
+    rows_total, cols_total = mesh_shape
+    smem = pl.BlockSpec(memory_space=pltpu.SMEM)
+    vmem = pl.BlockSpec(memory_space=pltpu.VMEM)
+    return pl.pallas_call(
         functools.partial(exchange_kernel, *mesh_shape),
-        out_shape=jax.ShapeDtypeStruct((2 * SIDE + 1,) + own.shape[1:], own.dtype),
-        in_specs=[pl.BlockSpec(memory_space=pl.ANY)],
-        out_specs=pl.BlockSpec(memory_space=pl.ANY),
+        out_shape=(
+            pltpu.VMEM((2 * SIDE + 1,) + own.shape[1:], own.dtype),
+            jax.ShapeDtypeStruct((2 * SIDE + 2, 1, 128), jnp.int32),
+        ),
+        in_specs=[smem, smem, pl.BlockSpec(memory_space=pl.ANY)],
+        out_specs=(vmem, vmem),
         scratch_shapes=[
+            pltpu.VMEM((rows_total * cols_total, 1, 128), jnp.int32),
             pltpu.SemaphoreType.DMA((8, CHUNKS)),
             pltpu.SemaphoreType.DMA((2 * SIDE + 1, CHUNKS)),
             pltpu.SemaphoreType.DMA,
+            pltpu.SemaphoreType.DMA((cols_total - 1,)),
+            pltpu.SemaphoreType.DMA((cols_total - 1,)),
+            pltpu.SemaphoreType.DMA((rows_total - 1,)),
+            pltpu.SemaphoreType.DMA((rows_total - 1,)),
         ],
-        compiler_params=pltpu.CompilerParams(collective_id=0, has_side_effects=True),
-    )(own)
-    return near
-
-
-def product_kernel(count, rows_here, slots, me_ref, table_ref, list_ref, near_ref, packed_ref, offset_ref, acc_ref):
+        compiler_params=pltpu.CompilerParams(collective_id=0, has_side_effects=True, vmem_limit_bytes=16 * 1024 * 1024),
+    )(colidx, counts, own)
+
+
+def product_kernel(count, rows_here, slots, me_ref, meta_ref, list_ref, near_ref, packed_ref, offset_ref, acc_ref):
     me = me_ref[0]
-    width = rows_here * slots + 1
+    entries = rows_here * slots
     total = count * rows_here
     band = 4 * H + 1
     first = me * rows_here
     tiles = rows_here * band
-
-    offset_ref[0, 0] = lax.fori_loop(0, me, lambda i, s: s + table_ref[i * width + width - 1], jnp.int32(0))
+    size = acc_ref.shape[1]
+
+    offset_ref[0, 0] = meta_ref[2 * SIDE + 1, 0, entries]
 
     def clear(q, carry):
         acc_ref[q] = jnp.zeros(acc_ref.shape[1:], acc_ref.dtype)
         return carry
 
-    lax.fori_loop(0, tiles, clear, 0, unroll=2)
+    lax.fori_loop(0, tiles, clear, 0, unroll=6)
 
     def wrapped(value):
         return lax.rem(value + total, total)
 
     def one(step, carry):
         a = step // slots
-        col = table_ref[me * width + step]
-        place = wrapped(col - first + SIDE * rows_here) * slots
-        left = near_ref[SIDE * rows_here * slots + step]
-        base = (col // rows_here) * width + (col % rows_here) * slots
+        col = meta_ref[SIDE, 0, step]
+        place = wrapped(col - first + SIDE * rows_here)
+        left = near_ref[SIDE, step]
+        source = place // rows_here
+        base = (place % rows_here) * slots
+        products = [
+            jnp.dot(left, near_ref[source, base + u], preferred_element_type=jnp.float32) for u in range(slots)
+        ]
         for u in range(slots):
-            f = wrapped(table_ref[base + u] - (first + a) + 2 * H)
-            q = a * band + f
-            acc_ref[q] += jnp.dot(left, near_ref[place + u], preferred_element_type=jnp.float32)
+            f = wrapped(meta_ref[source, 0, base + u] - (first + a) + 2 * H)
+            acc_ref[a * band + f] += products[u]
         return carry
 
-    lax.fori_loop(0, rows_here * slots, one, 0)
-
-    kept = table_ref[me * width + width - 1]
+    lax.fori_loop(0, entries, one, 0)
+
+    kept = meta_ref[SIDE, 0, entries]
 
     def pack(i, carry):
-        q = list_ref[i]
+        q = list_ref[0, 0, i]
         value = acc_ref[q].astype(packed_ref.dtype)
         packed_ref[i] = jnp.where(i < kept, value, jnp.zeros_like(value))
         return carry
 
-    lax.fori_loop(0, tiles, pack, 0, unroll=2)
+    lax.fori_loop(0, tiles, pack, 0, unroll=6)
 
 
 def shards(mesh_shape, blocks, colidx, counts, out_list):
@@ -191,10 +244,7 @@
     count = mesh_shape[0] * mesh_shape[1]
     tiles = out_list.shape[-1]
     me = (lax.axis_index("row") * mesh_shape[1] + lax.axis_index("col")).astype(jnp.int32)
-    meta = jnp.concatenate([colidx.reshape(-1), counts.reshape(-1)])
-    table = lax.all_gather(meta, ("row", "col"), tiled=True)
-    near = exchange(blocks, mesh_shape)
-    near = near.reshape(-1, size, size)
+    near, meta = exchange(blocks, colidx, counts, mesh_shape)
     smem = pl.BlockSpec(memory_space=pltpu.SMEM)
     vmem = pl.BlockSpec(memory_space=pltpu.VMEM)
     packed, offsets = pl.pallas_call(
@@ -206,8 +256,8 @@
         in_specs=[smem, smem, smem, vmem],
         out_specs=(vmem, smem),
         scratch_shapes=[pltpu.VMEM((tiles, size, size), jnp.float32)],
-        compiler_params=pltpu.CompilerParams(vmem_limit_bytes=40 * 1024 * 1024),
-    )(me.reshape(1), table, out_list.reshape(-1), near)
+        compiler_params=pltpu.CompilerParams(vmem_limit_bytes=32 * 1024 * 1024),
+    )(me.reshape(1), meta, out_list, near)
     return packed, offsets
 
 

time: 81.9 us -> 50.7 us (0.62)
  blocking collectives: 42 us -> 0 us
  Pallas kernels: 35 us -> 46.8 us
    unnamed x1 -> x0, blocking collectives: 42 us -> none
    pallas_call x1, Pallas kernels: 28.4 us -> 40.2 us  [exchange(): pl.pallas_call(functools.partial(exchange_kernel, *mesh_shape), out_shape...]
    unnamed x5 -> x6, local copies, waits for them, and re-layouts: 2.34 us -> 2.36 us
where the time goes in v2:
time: 50.7 us; the launch traced here: 50.5 us
  Pallas kernels  46.8 us (92%)
  local copies, waits for them, and re-layouts  2.36 us (5%)
  between operations  1.31 us (3%)
    pallas_call x1, Pallas kernels, exchange(): pl.pallas_call(functools.partial(exchange_kernel, *mesh_shape), out_shape...  40.2 us
    pallas_call x1, Pallas kernels, shards(): pl.pallas_call(functools.partial(product_kernel, count, rows_here, slots)...  6.61 us
    unnamed x6, local copies, waits for them, and re-layouts  2.36 us

profile of v2, /device:TPU:0, one launch (start us, length us, event | category | flops | bytes accessed | tf_op | source)
XLA Modules:
  0.0 50.5 jit_solution(309412643513658882)
XLA Ops:
  1.3 0.0 copy-start
  1.3 1.0 %copy-done = bf16[2,8,128,128]{3,2,1,0:T(8,128)(2,1)S(1)} copy-done((bf16[2,8,128,128]{3,2,1,0:T(8,128)(2,1)S(1)}, bf16[2,8,128,128]{3,2,1,0:T(8,128)(2,1)}, u32[]{:S(2)}) %copy-start) | copy-done | bytes 524312
  2.3 0.0 copy-start.1
  2.3 0.7 %copy-done.1 = s32[2,8]{1,0:T(2,128)S(1)} copy-done((s32[2,8]{1,0:T(2,128)S(1)}, s32[2,8]{1,0:T(2,128)}, u32[]{:S(2)}) %copy-start.1) | copy-done | bytes 88
  3.0 40.2 %shard_map.59 = (bf16[9,16,128,128]{3,2,1,0:T(8,128)(2,1)S(1)}, s32[10,1,128]{2,1,0:T(1,128)S(1)}) custom-call(s32[2,8]{1,0:T(2,128)S(1)} %copy-done.1, s32[1,1]{1,0:T(1,128)S(6)} %copy.6.count_ref, bf16[1,16,128,128]{3,2,1,0:T(8,128)(2,1)S(1)} %bitcast.2), custom_call_target="tpu_custom_call" | custom-call | tf_op jit(solution)/shard_map/pallas_call | solution.py:172
  43.2 0.0 copy-start.2
  43.3 0.6 %copy-done.2 = s32[1,1,66]{2,1,0:T(1,128)S(1)} copy-done((s32[1,1,66]{2,1,0:T(1,128)S(1)}, s32[1,1,66]{2,1,0:T(1,128)}, u32[]{:S(2)}) %copy-start.2) | copy-done | bytes 288
  43.9 6.6 %shard_map.60 = (bf16[66,128,128]{2,1,0:T(8,128)(2,1)}, s32[1,1]{1,0:T(1,128)}) custom-call(s32[1]{0:T(128)} %bitcast.me_ref, s32[10,1,128]{2,1,0:T(1,128)S(1)} %get-tuple-element.4.meta_ref, s32[1,1,66]{2,1,0:T(1,128)S(1)} %copy-done.2, bf16[9,16,128,128]{3,2,1,0:T(8,128)(2,1)S(1)} %get-tuple-element.5.near_ref), custom_call_target="tpu_custom_call" | custom-call | tf_op jit(solution)/shard_map/pallas_call | solution.py:250
Async XLA Ops:
  1.3 1.0 %copy-start = (bf16[2,8,128,128]{3,2,1,0:T(8,128)(2,1)S(1)}, bf16[2,8,128,128]{3,2,1,0:T(8,128)(2,1)}, u32[]{:S(2)}) copy-start(bf16[2,8,128,128]{3,2,1,0:T(8,128)(2,1)} %param.4) | copy-start | bytes 1572868
  2.3 0.7 %copy-start.1 = (s32[2,8]{1,0:T(2,128)S(1)}, s32[2,8]{1,0:T(2,128)}, u32[]{:S(2)}) copy-start(s32[2,8]{1,0:T(2,128)} %col_ref.1) | copy-start | bytes 196
  43.2 0.7 %copy-start.2 = (s32[1,1,66]{2,1,0:T(1,128)S(1)}, s32[1,1,66]{2,1,0:T(1,128)}, u32[]{:S(2)}) copy-start(s32[1,1,66]{2,1,0:T(1,128)} %list_ref.1) | copy-start | bytes 796

commit v3 on v2

--- a/solution.py
+++ b/solution.py
@@ -9,13 +9,17 @@
 
 H = 8
 CHUNKS = 4
+HALF = CHUNKS // 2
+X_ORDER = tuple(range(HALF, CHUNKS)) + tuple(range(HALF))
 SIDE = 4
 
 
 def exchange_kernel(
-    rows_total, cols_total, col_ref, count_ref, own_ref, near_ref, meta_ref,
-    table_ref, send_sem, recv_sem, own_sem, row_send, row_recv, grid_send, grid_recv,
+    rows_total, cols_total, col_hbm, count_ref, own_ref, near_ref, meta_ref,
+    table_ref, relay_ref, col_ref, send_sem, recv_sem, relay_sem, own_sem, col_sem, row_send, row_recv, grid_send, grid_recv,
 ):
+    col_copy = pltpu.make_async_copy(col_hbm, col_ref, col_sem)
+    col_copy.start()
     count = rows_total * cols_total
     me = lax.axis_index("row") * cols_total + lax.axis_index("col")
     core = me % 2
@@ -45,6 +49,9 @@
     for device in greeted:
         pl.semaphore_signal(barrier, inc=1, device_id=device, device_id_type=pl.DeviceIdType.MESH)
 
+    own_copy = pltpu.make_async_copy(own_ref.at[0], near_ref.at[SIDE], own_sem)
+    own_copy.start()
+    col_copy.wait()
     entries = col_ref.shape[0] * col_ref.shape[1]
     lane = lax.broadcasted_iota(jnp.int32, (1, 128), 1)
     row = jnp.where(lane == entries, count_ref[0, 0], 0)
@@ -85,27 +92,19 @@
     def forward(slot, c, lane, device, to_slot):
         copy(part(near_ref, slot, c), c, lane, device, to_slot).start()
 
-    own_copy = pltpu.make_async_copy(own_ref.at[0], near_ref.at[SIDE], own_sem)
-    own_copy.start()
-
     y_slot = SIDE + 4 * sign
     z_slot = SIDE - 4 * sign
     x_slot = SIDE + 2 * x_step
     x2_slot = SIDE - 2 * x_step
     to_partner = 2 * core - 1
-    for c in range(CHUNKS):
-        source = part(own_ref, 0, c)
-        copy(source, c, 0, y_dev, SIDE - 4 * sign).start()
-        copy(source, c, 1, x_dev, SIDE - 2 * x_step).start()
+    for j in range(cols_total - 1):
+        row_copy(j).start()
+    for i in range(CHUNKS):
+        copy(part(own_ref, 0, i), i, 0, y_dev, SIDE - 4 * sign).start()
+        c = X_ORDER[i]
+        copy(part(own_ref, 0, c), c, 1, x_dev, SIDE - 2 * x_step).start()
     for c in range(CHUNKS):
         copy(part(own_ref, 0, c), c, 2, partner, SIDE + to_partner).start()
-
-    for j in range(cols_total - 1):
-        row_copy(j).start()
-    for j in range(cols_total - 1):
-        row_copy(j).wait()
-    for j in range(rows_total - 1):
-        grid_copy(j).start()
 
     y_goes = (core == 0) == low
 
@@ -113,41 +112,70 @@
         wait_in(y_slot, c)
         forward(y_slot, c, 3, z_to, SIDE - 4 * sign)
 
-        @pl.when(type_a)
-        def _():
-            forward(y_slot, c, 4, x_dev, y_slot - 2 * x_step)
+        if c < HALF:
+            @pl.when(type_a)
+            def _():
+                forward(y_slot, c, 4, x_dev, y_slot - 2 * x_step)
 
         @pl.when(y_goes)
         def _():
             forward(y_slot, c, 6, partner, y_slot + to_partner)
 
+    def relay(c, lane, device):
+        return pltpu.make_async_remote_copy(
+            src_ref=part(near_ref, x_slot, c), dst_ref=relay_ref.at[c - HALF], send_sem=send_sem.at[lane, c],
+            recv_sem=relay_sem.at[c - HALF], device_id=place(device), device_id_type=pl.DeviceIdType.MESH)
+
     def x_arrived(c):
         wait_in(x_slot, c)
+        if c >= HALF:
+            @pl.when(type_a)
+            def _():
+                forward(x_slot, c, 8, y_dev, x_slot - 2 * y_step)
+
+            @pl.when(jnp.logical_not(type_a))
+            def _():
+                relay(c, 8, z_from).start()
         forward(x_slot, c, 5, partner, x_slot + to_partner)
 
     def z_arrived(c):
         wait_in(z_slot, c)
 
-        @pl.when(jnp.logical_not(type_a))
-        def _():
-            forward(z_slot, c, 4, x_dev, z_slot - 2 * x_step)
+        if c < HALF:
+            @pl.when(jnp.logical_not(type_a))
+            def _():
+                forward(z_slot, c, 4, x_dev, z_slot - 2 * x_step)
 
         @pl.when(jnp.logical_not(y_goes))
         def _():
             forward(z_slot, c, 6, partner, z_slot + to_partner)
 
+    def relay_arrived(c):
+        @pl.when(jnp.logical_not(type_a))
+        def _():
+            relay(c, 8, z_from).wait_recv()
+            copy(relay_ref.at[c - HALF], c, 9, y_dev, SIDE - 2 * x_step).start()
+
     def x2_arrived(c):
         wait_in(x2_slot, c)
         forward(x2_slot, c, 7, partner, x2_slot + to_partner)
 
-    for c in range(CHUNKS):
-        y_arrived(c)
-        x_arrived(c)
-        if c > 0:
-            z_arrived(c - 1)
+    for i in range(CHUNKS):
+        y_arrived(i)
+        x_arrived(X_ORDER[i])
+        if i > 0:
+            z_arrived(i - 1)
+            if i <= HALF:
+                relay_arrived(HALF + i - 1)
+        if i == 1:
+            for j in range(cols_total - 1):
+                row_copy(j).wait()
+            for j in range(rows_total - 1):
+                grid_copy(j).start()
     z_arrived(CHUNKS - 1)
-    for c in range(CHUNKS):
+    for c in range(HALF):
         x2_arrived(c)
+        x2_arrived(c + HALF)
     for c in range(CHUNKS):
         for odd in (SIDE - 3, SIDE - 1, SIDE + 1, SIDE + 3):
             wait_in(odd, c)
@@ -159,8 +187,13 @@
     index = lax.broadcasted_iota(jnp.int32, (count, 1, 128), 0)
     meta_ref[2 * SIDE + 1] = jnp.sum(jnp.where(index < me, table_ref[...], 0), axis=0)
     for c in range(CHUNKS):
-        for lane in range(8):
+        for lane in (0, 1, 2, 3, 5, 6, 7, 4 if c < HALF else 8):
             copy(part(own_ref, 0, c), c, lane, partner, SIDE).wait_send()
+
+    @pl.when(jnp.logical_not(type_a))
+    def _():
+        for c in range(HALF, CHUNKS):
+            copy(part(own_ref, 0, c), c, 9, partner, SIDE).wait_send()
 
 
 def exchange(blocks, colidx, counts, mesh_shape):
@@ -169,18 +202,23 @@
     rows_total, cols_total = mesh_shape
     smem = pl.BlockSpec(memory_space=pltpu.SMEM)
     vmem = pl.BlockSpec(memory_space=pltpu.VMEM)
+    hbm = pl.BlockSpec(memory_space=pltpu.HBM)
     return pl.pallas_call(
         functools.partial(exchange_kernel, *mesh_shape),
         out_shape=(
             pltpu.VMEM((2 * SIDE + 1,) + own.shape[1:], own.dtype),
             jax.ShapeDtypeStruct((2 * SIDE + 2, 1, 128), jnp.int32),
         ),
-        in_specs=[smem, smem, pl.BlockSpec(memory_space=pl.ANY)],
+        in_specs=[hbm, smem, hbm],
         out_specs=(vmem, vmem),
         scratch_shapes=[
             pltpu.VMEM((rows_total * cols_total, 1, 128), jnp.int32),
-            pltpu.SemaphoreType.DMA((8, CHUNKS)),
+            pltpu.VMEM((CHUNKS - HALF, rows_here * slots // CHUNKS, size, size), own.dtype),
+            pltpu.SMEM((rows_here, slots), jnp.int32),
+            pltpu.SemaphoreType.DMA((10, CHUNKS)),
             pltpu.SemaphoreType.DMA((2 * SIDE + 1, CHUNKS)),
+            pltpu.SemaphoreType.DMA((CHUNKS - HALF,)),
+            pltpu.SemaphoreType.DMA,
             pltpu.SemaphoreType.DMA,
             pltpu.SemaphoreType.DMA((cols_total - 1,)),
             pltpu.SemaphoreType.DMA((cols_total - 1,)),
@@ -188,10 +226,12 @@
             pltpu.SemaphoreType.DMA((rows_total - 1,)),
         ],
         compiler_params=pltpu.CompilerParams(collective_id=0, has_side_effects=True, vmem_limit_bytes=16 * 1024 * 1024),
-    )(colidx, counts, own)
-
-
-def product_kernel(count, rows_here, slots, me_ref, meta_ref, list_ref, near_ref, packed_ref, offset_ref, acc_ref):
+    )(pltpu.with_memory_space_constraint(colidx, pltpu.HBM), counts, pltpu.with_memory_space_constraint(own, pltpu.HBM))
+
+
+def product_kernel(count, rows_here, slots, me_ref, meta_ref, list_hbm, near_ref, packed_ref, offset_ref, acc_ref, list_ref, list_sem):
+    list_copy = pltpu.make_async_copy(list_hbm, list_ref, list_sem)
+    list_copy.start()
     me = me_ref[0]
     entries = rows_here * slots
     total = count * rows_here
@@ -218,16 +258,16 @@
         left = near_ref[SIDE, step]
         source = place // rows_here
         base = (place % rows_here) * slots
-        products = [
-            jnp.dot(left, near_ref[source, base + u], preferred_element_type=jnp.float32) for u in range(slots)
-        ]
+        right = jnp.concatenate([near_ref[source, base + u] for u in range(slots)], axis=1)
+        product = jnp.dot(left, right, preferred_element_type=jnp.float32)
         for u in range(slots):
             f = wrapped(meta_ref[source, 0, base + u] - (first + a) + 2 * H)
-            acc_ref[a * band + f] += products[u]
+            acc_ref[a * band + f] += product[:, u * size:(u + 1) * size]
         return carry
 
     lax.fori_loop(0, entries, one, 0)
 
+    list_copy.wait()
     kept = meta_ref[SIDE, 0, entries]
 
     def pack(i, carry):
@@ -253,11 +293,15 @@
             jax.ShapeDtypeStruct((tiles, size, size), jnp.bfloat16),
             jax.ShapeDtypeStruct((1, 1), jnp.int32),
         ),
-        in_specs=[smem, smem, smem, vmem],
+        in_specs=[smem, smem, pl.BlockSpec(memory_space=pltpu.HBM), vmem],
         out_specs=(vmem, smem),
-        scratch_shapes=[pltpu.VMEM((tiles, size, size), jnp.float32)],
+        scratch_shapes=[
+            pltpu.VMEM((tiles, size, size), jnp.float32),
+            pltpu.SMEM(out_list.shape, jnp.int32),
+            pltpu.SemaphoreType.DMA,
+        ],
         compiler_params=pltpu.CompilerParams(vmem_limit_bytes=32 * 1024 * 1024),
-    )(me.reshape(1), meta, out_list, near)
+    )(me.reshape(1), meta, pltpu.with_memory_space_constraint(out_list, pltpu.HBM), near)
     return packed, offsets
 
 

time: 50.7 us -> 40.6 us (0.80)
  the two profiles are of different devices: /device:TPU:0 before, /device:TPU:3 now
where the time goes in v3:
time: 40.6 us; the launch traced here: 40.4 us
  Pallas kernels  39.1 us (96%)
  between operations  1.29 us (3%)
    pallas_call x1, Pallas kernels, exchange(): pl.pallas_call(functools.partial(exchange_kernel, *mesh_shape), out_shape...  32.4 us
    pallas_call x1, Pallas kernels, shards(): pl.pallas_call(functools.partial(product_kernel, count, rows_here, slots)...  6.67 us

profile of v3, /device:TPU:3, one launch (start us, length us, event | category | flops | bytes accessed | tf_op | source)
XLA Modules:
  0.0 40.4 jit_solution(3162088124915923786)
XLA Ops:
  1.3 32.4 %shard_map.59 = (bf16[9,16,128,128]{3,2,1,0:T(8,128)(2,1)S(1)}, s32[10,1,128]{2,1,0:T(1,128)S(1)}) custom-call(s32[2,8]{1,0:T(2,128)} %col_hbm.1, s32[1,1]{1,0:T(1,128)S(6)} %copy.6.count_ref, bf16[1,16,128,128]{3,2,1,0:T(8,128)(2,1)} %bitcast.2), custom_call_target="tpu_custom_call" | custom-call | tf_op jit(solution)/shard_map/pallas_call | solution.py:206
  33.7 6.7 %shard_map.60 = (bf16[66,128,128]{2,1,0:T(8,128)(2,1)}, s32[1,1]{1,0:T(1,128)}) custom-call(s32[1]{0:T(128)} %bitcast.me_ref, s32[10,1,128]{2,1,0:T(1,128)S(1)} %get-tuple-element.4.meta_ref, s32[1,1,66]{2,1,0:T(1,128)} %list_hbm.1, bf16[9,16,128,128]{3,2,1,0:T(8,128)(2,1)S(1)} %get-tuple-element.5.near_ref), custom_call_target="tpu_custom_call" | custom-call | tf_op jit(solution)/shard_map/pallas_call | solution.py:290

commit v4 on v3

--- a/solution.py
+++ b/solution.py
@@ -229,7 +229,12 @@
     )(pltpu.with_memory_space_constraint(colidx, pltpu.HBM), counts, pltpu.with_memory_space_constraint(own, pltpu.HBM))
 
 
-def product_kernel(count, rows_here, slots, me_ref, meta_ref, list_hbm, near_ref, packed_ref, offset_ref, acc_ref, list_ref, list_sem):
+def product_kernel(
+    count, rows_here, slots, me_ref, meta_vmem, list_hbm, near_ref, packed_ref, offset_ref,
+    acc_ref, out_ref, meta_ref, list_ref, meta_sem, list_sem, out_sem,
+):
+    meta_copy = pltpu.make_async_copy(meta_vmem, meta_ref, meta_sem)
+    meta_copy.start()
     list_copy = pltpu.make_async_copy(list_hbm, list_ref, list_sem)
     list_copy.start()
     me = me_ref[0]
@@ -240,13 +245,14 @@
     tiles = rows_here * band
     size = acc_ref.shape[1]
 
-    offset_ref[0, 0] = meta_ref[2 * SIDE + 1, 0, entries]
-
     def clear(q, carry):
         acc_ref[q] = jnp.zeros(acc_ref.shape[1:], acc_ref.dtype)
         return carry
 
     lax.fori_loop(0, tiles, clear, 0, unroll=6)
+
+    meta_copy.wait()
+    offset_ref[0, 0] = meta_ref[2 * SIDE + 1, 0, entries]
 
     def wrapped(value):
         return lax.rem(value + total, total)
@@ -265,18 +271,26 @@
             acc_ref[a * band + f] += product[:, u * size:(u + 1) * size]
         return carry
 
-    lax.fori_loop(0, entries, one, 0)
+    lax.fori_loop(0, entries, one, 0, unroll=True)
 
     list_copy.wait()
     kept = meta_ref[SIDE, 0, entries]
 
     def pack(i, carry):
         q = list_ref[0, 0, i]
-        value = acc_ref[q].astype(packed_ref.dtype)
-        packed_ref[i] = jnp.where(i < kept, value, jnp.zeros_like(value))
+        value = acc_ref[q].astype(out_ref.dtype)
+        out_ref[i] = jnp.where(i < kept, value, jnp.zeros_like(value))
         return carry
 
-    lax.fori_loop(0, tiles, pack, 0, unroll=6)
+    group = band // 3
+    writes = []
+    for g in range(tiles // group):
+        lax.fori_loop(g * group, (g + 1) * group, pack, 0, unroll=True)
+        span = pl.ds(g * group, group)
+        writes.append(pltpu.make_async_copy(out_ref.at[span], packed_ref.at[span], out_sem.at[g]))
+        writes[-1].start()
+    for write in writes:
+        write.wait()
 
 
 def shards(mesh_shape, blocks, colidx, counts, out_list):
@@ -287,18 +301,23 @@
     near, meta = exchange(blocks, colidx, counts, mesh_shape)
     smem = pl.BlockSpec(memory_space=pltpu.SMEM)
     vmem = pl.BlockSpec(memory_space=pltpu.VMEM)
+    hbm = pl.BlockSpec(memory_space=pltpu.HBM)
     packed, offsets = pl.pallas_call(
         functools.partial(product_kernel, count, rows_here, slots),
         out_shape=(
             jax.ShapeDtypeStruct((tiles, size, size), jnp.bfloat16),
             jax.ShapeDtypeStruct((1, 1), jnp.int32),
         ),
-        in_specs=[smem, smem, pl.BlockSpec(memory_space=pltpu.HBM), vmem],
-        out_specs=(vmem, smem),
+        in_specs=[smem, vmem, hbm, vmem],
+        out_specs=(hbm, smem),
         scratch_shapes=[
             pltpu.VMEM((tiles, size, size), jnp.float32),
+            pltpu.VMEM((tiles, size, size), jnp.bfloat16),
+            pltpu.SMEM(meta.shape, jnp.int32),
             pltpu.SMEM(out_list.shape, jnp.int32),
             pltpu.SemaphoreType.DMA,
+            pltpu.SemaphoreType.DMA,
+            pltpu.SemaphoreType.DMA((3 * rows_here,)),
         ],
         compiler_params=pltpu.CompilerParams(vmem_limit_bytes=32 * 1024 * 1024),
     )(me.reshape(1), meta, pltpu.with_memory_space_constraint(out_list, pltpu.HBM), near)

time: 40.6 us -> 37.9 us (0.933)
  Pallas kernels: 39.1 us -> 36.4 us
    pallas_call x1, Pallas kernels: 6.67 us -> 4 us  [shards(): pl.pallas_call(functools.partial(product_kernel, count, rows_here, slots)...]
where the time goes in v4:
time: 37.9 us; the launch traced here: 37.7 us
  Pallas kernels  36.4 us (96%)
  between operations  1.29 us (3%)
    pallas_call x1, Pallas kernels, exchange(): pl.pallas_call(functools.partial(exchange_kernel, *mesh_shape), out_shape...  32.4 us
    pallas_call x1, Pallas kernels, shards(): pl.pallas_call(functools.partial(product_kernel, count, rows_here, slots)...  4 us

profile of v4, /device:TPU:3, one launch (start us, length us, event | category | flops | bytes accessed | tf_op | source)
XLA Modules:
  0.0 37.7 jit_solution(15693611590027369339)
XLA Ops:
  1.3 32.4 %shard_map.59 = (bf16[9,16,128,128]{3,2,1,0:T(8,128)(2,1)S(1)}, s32[10,1,128]{2,1,0:T(1,128)S(1)}) custom-call(s32[2,8]{1,0:T(2,128)} %col_hbm.1, s32[1,1]{1,0:T(1,128)S(6)} %copy.6.count_ref, bf16[1,16,128,128]{3,2,1,0:T(8,128)(2,1)} %bitcast.2), custom_call_target="tpu_custom_call" | custom-call | tf_op jit(solution)/shard_map/pallas_call | solution.py:206
  33.7 4.0 %shard_map.60 = (bf16[66,128,128]{2,1,0:T(8,128)(2,1)}, s32[1,1]{1,0:T(1,128)}) custom-call(s32[1]{0:T(128)} %bitcast.me_ref, s32[10,1,128]{2,1,0:T(1,128)S(1)} %get-tuple-element.4.meta_vmem, s32[1,1,66]{2,1,0:T(1,128)} %list_hbm.1, bf16[9,16,128,128]{3,2,1,0:T(8,128)(2,1)S(1)} %get-tuple-element.5.near_ref), custom_call_target="tpu_custom_call" | custom-call | tf_op jit(solution)/shard_map/pallas_call | solution.py:305
